TPU v7x, 1024 devices: a whole 8x8x8 slice. The times are simulated.
1024 devices in a mesh: mp: 32 (over x, z_hi, core), replica: 32 (over y, z_lo).
Axes of the slice: x: 8, y: 8, z: 8 (z_hi: 2, z_lo: 4; z = z_hi * 4 + z_lo), core: 2. Of those that a mesh axis runs over, the one named last changes fastest.
Arguments:
- tables: bfloat16 [256, 512, 128], P('mp'), may hold values from -6 to 6
- feature_ids: int32 [24576, 256, 4], P('replica', 'mp'), may hold values from 0 to 511
- bag_lengths: int32 [24576, 256], P('replica', 'mp'), may hold values from 1 to 4
- reduce_weight: bfloat16 [32768, 256], P('mp'), may hold values from -0.03125 to 0.03125
- expand_weight: bfloat16 [32768, 256], P('mp'), may hold values from -0.375 to 0.375
- cross_bias: float32 [32768], P('mp'), may hold values from -3 to 3
- cotangent: bfloat16 [24576, 32768], P('replica', 'mp'), may hold values from -6 to 6
Outputs:
- crossed: bfloat16 [24576, 32768], P('replica', 'mp')
- grad_reduce: float32 [32768, 256], P(('mp', 'replica'))
- grad_expand: float32 [32768, 256], P(('mp', 'replica'))
- grad_bias: float32 [32768], P(('mp', 'replica'))
- grad_tables: float32 [256, 512, 128], P('mp', 'replica')
All inputs are finite; a program needn't handle non-finite values.
Results may differ from a plain program's by a relative error of at most 0.0058.
Values may be sent and summed in bfloat16 or wider, within the bound.
A program may use at most 32 MiB of HBM per device.

v0:
```python
import jax
import jax.numpy as jnp
from jax import lax
from jax.sharding import PartitionSpec as P


def bag_counts(id_cols, len_col, row_count):
    live = jnp.arange(id_cols.shape[1], dtype=jnp.int32)[None, :] < len_col[:, None]
    match = id_cols[:, :, None] == jnp.arange(row_count, dtype=jnp.int32)[None, None, :]
    return jnp.sum(jnp.where(match & live[:, :, None], jnp.float32(1.0), jnp.float32(0.0)), axis=1)


def pool_table(table, id_cols, len_col):
    counts = bag_counts(id_cols, len_col, table.shape[0]).astype(jnp.bfloat16)
    total = jnp.dot(counts, table, preferred_element_type=jnp.float32)
    return total / len_col[:, None].astype(jnp.float32)


def spread_table(grad_cols, id_cols, len_col, row_count):
    counts = bag_counts(id_cols, len_col, row_count)
    scaled = grad_cols * (jnp.float32(1.0) / len_col[:, None].astype(jnp.float32))
    return jnp.dot(
        counts.T, scaled, preferred_element_type=jnp.float32, precision=lax.Precision.HIGHEST
    )


def rank_total(partial_value):
    return lax.psum(partial_value, "mp").astype(jnp.bfloat16)


def body(tables, feature_ids, bag_lengths, reduce_weight, expand_weight, cross_bias, cotangent):
    local_tables = tables.shape[0]
    row_count = tables.shape[1]
    width = tables.shape[2]
    group = feature_ids.shape[0]
    ids_t = jnp.transpose(feature_ids, (1, 0, 2))
    lens_t = bag_lengths.T
    pooled = lax.map(lambda a: pool_table(a[0], a[1], a[2]), (tables, ids_t, lens_t))
    pooled = (
        jnp.transpose(pooled, (1, 0, 2)).reshape(group, local_tables * width).astype(jnp.bfloat16)
    )
    low = rank_total(jnp.dot(pooled, reduce_weight, preferred_element_type=jnp.float32))
    inner = jnp.dot(low, expand_weight.T, preferred_element_type=jnp.float32) + cross_bias[None, :]
    pooled_f = pooled.astype(jnp.float32)
    crossed = (pooled_f * inner + pooled_f).astype(jnp.bfloat16)
    grad_f = cotangent.astype(jnp.float32)
    grad_inner = grad_f * pooled_f
    grad_inner_b = grad_inner.astype(jnp.bfloat16)
    grad_low = rank_total(jnp.dot(grad_inner_b, expand_weight, preferred_element_type=jnp.float32))
    grad_pooled = grad_f * (inner + 1.0) + jnp.dot(
        grad_low, reduce_weight.T, preferred_element_type=jnp.float32
    )
    part_expand = jnp.dot(grad_inner_b.T, low, preferred_element_type=jnp.float32)
    part_reduce = jnp.dot(pooled.T, grad_low, preferred_element_type=jnp.float32)
    part_bias = jnp.sum(grad_inner, axis=0)
    grad_reduce, grad_expand, grad_bias = (
        lax.psum_scatter(part_reduce, "replica", scatter_dimension=0, tiled=True),
        lax.psum_scatter(part_expand, "replica", scatter_dimension=0, tiled=True),
        lax.psum_scatter(part_bias, "replica", scatter_dimension=0, tiled=True),
    )
    grad_cols = jnp.transpose(grad_pooled.reshape(group, local_tables, width), (1, 0, 2))
    part_tables = lax.map(
        lambda a: spread_table(a[0], a[1], a[2], row_count), (grad_cols, ids_t, lens_t)
    )
    grad_tables = lax.psum_scatter(part_tables, "replica", scatter_dimension=1, tiled=True)
    return (crossed, grad_reduce, grad_expand, grad_bias, grad_tables)


def solution(mesh):
    in_specs = (
        P("mp", None, None),
        P("replica", "mp", None),
        P("replica", "mp"),
        P("mp", None),
        P("mp", None),
        P("mp"),
        P("replica", "mp"),
    )
    out_specs = (
        P("replica", "mp"),
        P(("mp", "replica"), None),
        P(("mp", "replica"), None),
        P(("mp", "replica")),
        P("mp", "replica", None),
    )
    return jax.shard_map(body, mesh=mesh, in_specs=in_specs, out_specs=out_specs, check_vma=False)
```

profile of v0, /device:TPU:4, one launch (start us, length us, event | category | flops | bytes accessed | tf_op | source)
XLA Modules:
  0.0 767.0 jit_solution(9031511085983225936)
XLA Ops:
  7.2 42.0 %while.20 = (s32[]{:T(128)}, bf16[8,768,128]{2,1,0:T(8,128)(2,1)}, s32[8,768,4]{1,2,0:T(4,128)}, s32[8,768]{1,0:T(8,128)}, bf16[8,512,128]{2,1,0:T(8,128)(2,1)}, /*index=5*/s32[]{:T(128)}) while((s32[]{:T(128)}, bf16[8,768,128]{2,1,0:T(8,128)(2,1)}, s32[8,768,4]{1,2,0:T(4,128)}, s32[8,768]{1,0:T(8,128)}, bf16[8,512,128]{2,1,0:T(8,128)(2,1)}, ...), condition=%wide.region_2.3_spmd, body=%wide.region_0.2_spmd.sunk | while | flops 106663680 | bytes 2159701 | solution.py:38
  8.9 1.8 select_reduce_fusion.4
  10.7 2.0 fusion.54
  14.1 1.8 select_reduce_fusion.4
  15.9 2.0 fusion.54
  19.3 1.8 select_reduce_fusion.4
  21.1 1.9 fusion.54
  24.6 1.8 select_reduce_fusion.4
  26.3 2.0 fusion.54
  31.6 2.0 fusion.54
  36.8 2.0 fusion.54
  42.0 2.0 fusion.54
  47.2 2.0 fusion.54
  49.2 2.1 fusion.25
  52.8 183.0 %all-reduce.3 = (bf16[768,256]{1,0:T(8,128)(2,1)}, bf16[768,256]{1,0:T(8,128)(2,1)}) all-reduce(f32[768,256]{1,0:T(8,128)} %fusion.19, f32[768,256]{1,0:T(8,128)S(1)} %fusion.25), channel_id=1, replica_groups=mesh['mp'=32,'replica'=32] {'mp'}, use_global_device_ids=true, to_apply=%region_3.4 | all-reduce | flops 393216 | bytes 2359296 | tf_op jit(solution)/shard_map/psum | solution.py:28
  235.8 3.1 fusion.23
  239.1 3.1 fusion.17
  242.2 3.5 fusion.15
  246.5 1.9 copy.40
  248.4 61.4 %while.21 = (s32[]{:T(128)}, f32[8,512,128]{2,1,0:T(8,128)}, s32[8,768,4]{1,2,0:T(4,128)}, s32[8,768]{1,0:T(8,128)}, f32[8,768,128]{2,1,0:T(8,128)}, /*index=5*/s32[]{:T(128)}) while((s32[]{:T(128)}, f32[8,512,128]{2,1,0:T(8,128)}, s32[8,768,4]{1,2,0:T(4,128)}, s32[8,768]{1,0:T(8,128)}, f32[8,768,128]{2,1,0:T(8,128)}, ...), condition=%wide.region_11.12_spmd, body=%wide.region_9.11_spmd.sunk | while | flops 609980928 | bytes 3863637 | solution.py:62
  251.6 4.5 fusion.56
  259.2 4.5 fusion.56
  266.9 4.5 fusion.56
  274.6 4.5 fusion.56
  282.3 4.5 fusion.56
  289.9 4.5 fusion.56
  297.6 4.5 fusion.56
  305.3 4.5 fusion.56
  311.7 82.8 %all-reduce = f32[1024]{0:T(1024)S(1)} all-reduce(f32[1024]{0:T(1024)S(1)} %get-tuple-element.83), channel_id=4, replica_groups=mesh['mp'=32,'replica'=32] {'replica'}, use_global_device_ids=true, to_apply=%region_8.9.clone | all-reduce | flops 1024 | bytes 8192
  395.1 30.1 %reduce-scatter.6.cloned.1.call-done = f32[32,256]{1,0:T(8,128)} async-done(((f32[1024,256]{1,0:T(8,128)}), f32[32,256]{1,0:T(8,128)}) %reduce-scatter.6.cloned.1.call-update) | async-done | bytes 32784 | tf_op jit(solution)/shard_map/reduce_scatter | solution.py:58
  425.3 166.5 %reduce-scatter.4.cloned.1.call-done = f32[32,256]{1,0:T(8,128)} async-done(((f32[1024,256]{1,0:T(8,128)}), f32[32,256]{1,0:T(8,128)}) %reduce-scatter.4.cloned.1.call-update) | async-done | bytes 32784 | tf_op jit(solution)/shard_map/reduce_scatter | solution.py:57
  591.7 168.7 %reduce-scatter.8.cloned.1.call-done = f32[8,16,128]{2,1,0:T(8,128)} async-done(((f32[8,512,128]{2,1,0:T(8,128)}), f32[8,16,128]{2,1,0:T(8,128)}) %reduce-scatter.8.cloned.1.call-update) | async-done | bytes 65552 | tf_op jit(solution)/shard_map/reduce_scatter | solution.py:65
  (102 shorter events, 48.7 us)
Async XLA Ops:
  7.2 42.0 %copy-start = (bf16[1024,256]{1,0:T(8,128)(2,1)S(1)}, bf16[1024,256]{1,0:T(8,128)(2,1)}, u32[]{:S(2)}) copy-start(bf16[1024,256]{1,0:T(8,128)(2,1)} %param.15) | copy-start | bytes 1572868
  7.2 418.1 %reduce-scatter.6.cloned.1.call-start = ((), (), s32[]{:S(2)}) async-start(), calls=%async_computation.4 | async-start | bytes 1081344 | tf_op jit(solution)/shard_map/reduce_scatter | solution.py:58
  7.2 42.0 %copy-start.1 = (bf16[768,1024]{1,0:T(8,128)(2,1)S(1)}, bf16[768,1024]{1,0:T(8,128)(2,1)}, u32[]{:S(2)}) copy-start(bf16[768,1024]{1,0:T(8,128)(2,1)} %param.17) | copy-start | bytes 4718596
  49.2 2.2 copy-start.2
  49.2 2.2 copy-start.3
  235.8 3.2 copy-start.4
  239.0 352.7 %reduce-scatter.4.cloned.1.call-start = ((), (), s32[]{:S(2)}) async-start(), calls=%async_computation.3 | async-start | bytes 1081344 | tf_op jit(solution)/shard_map/reduce_scatter | solution.py:57
  239.0 3.2 copy-start.5
  239.1 3.2 copy-start.6
  242.2 518.3 %reduce-scatter.8.cloned.1.call-start = ((), (), s32[]{:S(2)}) async-start(), calls=%async_computation.5 | async-start | bytes 2162688 | tf_op jit(solution)/shard_map/reduce_scatter | solution.py:65
Sparse Core Ops, SparseCore 0:
  239.1 186.1 reduce-scatter.5
  429.6 162.0 reduce-scatter.3
  595.7 164.7 reduce-scatter.7
where the time goes:
time: 769 us; the launch traced here: 767 us
  waiting for transfers between devices  365 us (47%)
  blocking collectives  266 us (35%)
  matrix products  65.5 us (9%)
  other arithmetic  27.8 us (4%)
  local copies, waits for them, and re-layouts  27.4 us (4%)
  between operations  14.5 us (2%)
    psum x1, blocking collectives, rank_total(): return lax.psum(partial_value, 'mp').astype(jnp.bfloat16)  183 us
    reduce_scatter x1, waiting for transfers between devices, body(): lax.psum_scatter(part_tables, 'replica', scatter_dimension=1, tiled=True)  169 us
    reduce_scatter x1, waiting for transfers between devices, body(): lax.psum_scatter(part_reduce, 'replica', scatter_dimension=0, tiled=True)  166 us
    unnamed x1, blocking collectives  82.8 us
    dot_general x8, matrix products, spread_table(): jnp.dot(counts.T, scaled, preferred_element_type=jnp.float32, precision=l...  35.8 us
    reduce_scatter x1, waiting for transfers between devices, body(): lax.psum_scatter(part_expand, 'replica', scatter_dimension=0, tiled=True)  30.1 us
    reduce_sum x16, other arithmetic, bag_counts(): jnp.sum(jnp.where(match & live[:, :, None], jnp.float32(1.0), jnp.float32...  27.6 us
    dot_general x8, matrix products, pool_table(): total = jnp.dot(counts, table, preferred_element_type=jnp.float32)  15.7 us
  transfers between devices with their start and end apart: 3, of which 3 were waited for; matrix products, arithmetic and copies ran while one was open for 9% of the time, Pallas kernels for 0%

commit v1 on v0

v1 whole, which is shorter than its diff:
```python
import jax
import jax.numpy as jnp
from jax import lax
from jax.experimental import pallas as pl
from jax.experimental.pallas import tpu as pltpu
from jax.sharding import PartitionSpec as P

NX, NZH, NCORE = 8, 2, 2
NY, NZL = 8, 4
NREP = NY * NZL
TABLES, ROWS, EMB, HOT = 8, 512, 128, 4
FEATURES, RANK = TABLES * EMB, 256
GROUP = 768
HALF = GROUP // NCORE
CHUNK = HALF // NX
PIECES = 4
TPP = 4
WIDE = 64
TALL = 80
MESH = pl.DeviceIdType.MESH
BF16 = jnp.bfloat16
F32 = jnp.float32


def hops(part, way, n):
    far = n // 2
    return far if part % 2 == way else n - 1 - far


def dot(a, b, dims):
    return lax.dot_general(a, b, (dims, ((), ())), preferred_element_type=F32)


class Links:
    def __init__(self, send_sems, recv_sems):
        self.send_sems, self.recv_sems = send_sems, recv_sems
        self.used = 0
        self.sent = []

    def copy(self, src, dst, device):
        i = self.used
        self.used += 1
        made = pltpu.make_async_remote_copy(
            src_ref=src,
            dst_ref=dst,
            send_sem=self.send_sems.at[i],
            recv_sem=self.recv_sems.at[i],
            device_id=device,
            device_id_type=MESH,
        )
        made.start()
        self.sent.append(made)
        return made


COPIES = 1 + 14 + 2 + 14 + 16 + 7 * PIECES + 3 * PIECES


def kernel(
    ids_ref, lens_ref, tables_ref, rw_ref, ew_ref, bias_ref, cot_ref,
    crossed_ref, reduce_ref, expand_ref, gbias_ref, gtables_ref,
    counts, tabs_t, pooled, pooled_t, gb, gb_t, spread, inv_col, inv_row, biases,
    core_send, core_recv, rank_own, rank_send, rank_recv, zh_send, zh_recv, low,
    own_a, own_b, own_c, own_d, send_a, send_bcd, recv_a, recv_bcd, zl_send_a, zl_send, zl_recv_a, zl_recv,
    send_sems, recv_sems,
):
    m, r = lax.axis_index("mp"), lax.axis_index("replica")
    core, zh, x = lax.rem(m, 2), lax.rem(m // 2, 2), m // 4
    y, zl = r // NZL, lax.rem(r, NZL)

    def mp_at(xx, zz, cc):
        return {"mp": (xx * NZH + zz) * NCORE + cc}

    def rep_at(yy, zz):
        return {"replica": yy * NZL + zz}

    x_side = (mp_at(lax.rem(x + 1, NX), zh, core), mp_at(lax.rem(x + NX - 1, NX), zh, core))
    y_side = (rep_at(lax.rem(y + 1, NY), zl), rep_at(lax.rem(y + NY - 1, NY), zl))
    other_core, other_zh = mp_at(x, zh, 1 - core), mp_at(x, 1 - zh, core)
    zl_peer = [rep_at(y, lax.rem(zl + o, NZL)) for o in range(1, NZL)]

    barrier = pltpu.get_barrier_semaphore()
    greeted = [*x_side, *y_side, other_core, other_zh, *zl_peer]
    for device in greeted:
        pl.semaphore_signal(barrier, inc=1, device_id=device, device_id_type=MESH)

    links = Links(send_sems, recv_sems)

    inv_row[...] = 1.0 / lens_ref[...].astype(F32)
    inv_col[...] = jnp.transpose(inv_row[...])
    biases[...] = jnp.zeros_like(biases)

    def make_tab(t, carry):
        tabs_t[t] = jnp.transpose(tables_ref[t])
        return carry

    lax.fori_loop(0, TABLES, make_tab, 0)

    def half(start):
        span = pl.ds(pl.multiple_of(start, 128), HALF)
        row_of = lax.broadcasted_iota(jnp.int32, (64, HALF), 0)

        def table(t, carry):
            lens = lens_ref[pl.ds(t, 1), span]
            picks = []
            for j in range(HOT):
                picks.append(jnp.where(lens > j, ids_ref[t, j : j + 1, span], -1))
            for c in range(ROWS // 64):
                total = jnp.zeros((64, HALF), F32)
                for j in range(HOT):
                    total = jnp.where(row_of == picks[j] - 64 * c, total + 1.0, total)
                counts[t, 64 * c : 64 * c + 64, span] = total.astype(BF16)
            columns = pl.ds(pl.multiple_of(t * EMB, EMB), EMB)
            sums = dot(tabs_t[t], counts[t, :, span], ((1,), (0,)))
            mean_t = (sums * inv_row[pl.ds(t, 1), span]).astype(BF16)
            pooled_t[columns, span] = mean_t
            mean = jnp.transpose(mean_t)
            pooled[pl.ds(start, HALF), columns] = mean
            grad = cot_ref[pl.ds(start, HALF), columns].astype(F32) * mean.astype(F32)
            gb[pl.ds(start, HALF), columns] = grad.astype(BF16)
            biases[pl.ds(t, 1), :] += jnp.sum(grad, axis=0, keepdims=True)
            return carry

        lax.fori_loop(0, TABLES, table, 0)
        rows = pl.ds(start, HALF)
        return (
            dot(pooled[rows, :], rw_ref[...], ((1,), (0,))),
            dot(gb[rows, :], ew_ref[...], ((1,), (0,))),
        )

    theirs = pl.multiple_of((1 - core) * HALF, HALF)
    mine = pl.multiple_of(core * HALF, HALF)
    parts = half(theirs)
    core_send[0] = parts[0]
    core_send[1] = parts[1]
    pl.semaphore_wait(barrier, len(greeted))
    from_core = links.copy(core_send, core_recv, other_core)
    parts = half(mine)
    from_core.wait_recv()
    for p in range(2):
        rank_own[p] = (parts[p] + core_recv[p]).reshape(NX, CHUNK, RANK)

    def reduce_chain(part, n, me, own, send, recv, sides):
        count = [hops(part, way, n) for way in range(2)]
        flights = [[], []]
        for step in range(max(count)):
            for way in range(2):
                if step >= count[way]:
                    continue
                d = count[way] - step
                dest = lax.rem(me + d, n) if way == 0 else lax.rem(me + n - d, n)
                value = own(dest)
                if step > 0:
                    flights[way][step - 1].wait_recv()
                    value = value + recv(way, step - 1)[...].astype(F32)
                send(way, step)[...] = value.astype(BF16)
                flights[way].append(links.copy(send(way, step), recv(way, step), sides[way]))
            yield
        for way in range(2):
            flights[way][-1].wait_recv()
        yield [recv(way, count[way] - 1) for way in range(2)]

    rank_chains = [
        reduce_chain(
            p, NX, x,
            lambda dest, p=p: rank_own[p, dest],
            lambda way, step, p=p: rank_send.at[p, way, step],
            lambda way, step, p=p: rank_recv.at[p, way, step],
            x_side,
        )
        for p in range(2)
    ]

    def flip(t):
        gb_t[t * EMB : (t + 1) * EMB, :] = jnp.transpose(gb[:, t * EMB : (t + 1) * EMB])

    for step in range(NX // 2):
        for p in range(2):
            next(rank_chains[p])
        flip(2 * step)
        flip(2 * step + 1)

    summed = []
    swaps = []
    for p in range(2):
        arrived = next(rank_chains[p])
        value = rank_own[p, x] + arrived[0][...].astype(F32) + arrived[1][...].astype(F32)
        summed.append(value)
        zh_send[p] = value.astype(BF16)
        swaps.append(links.copy(zh_send.at[p], zh_recv.at[p], other_zh))

    def block(p, xx):
        return low.at[p, pl.ds(pl.multiple_of(mine + xx * CHUNK, 16), CHUNK), :]

    handed = [[], []]
    gathers = [[[], []], [[], []]]
    for p in range(2):
        swaps[p].wait_recv()
        block(p, x)[...] = (summed[p] + zh_recv[p].astype(F32)).astype(BF16)
        for way in range(2):
            gathers[p][way].append(links.copy(block(p, x), block(p, x), x_side[way]))
        handed[p].append(links.copy(block(p, x), block(p, x), other_core))
    for step in range(1, NX // 2 + 1):
        for p in range(2):
            for way in range(2):
                count = hops(p, way, NX)
                if step > count:
                    continue
                source = lax.rem(x + NX - step, NX) if way == 0 else lax.rem(x + step, NX)
                gathers[p][way][step - 1].wait_recv()
                if step < count:
                    gathers[p][way].append(
                        links.copy(block(p, source), block(p, source), x_side[way])
                    )
                handed[p].append(links.copy(block(p, source), block(p, source), other_core))

    owns = [own_a, own_b, own_c, own_d]

    def weight_piece(p, left, right):
        for i in range(TABLES // 2):
            value = dot(left[256 * i : 256 * i + 256, :], right, ((1,), (0,)))
            value = value.reshape(8, 32, RANK)
            owns[p][8 * i : 8 * i + 8, 0:32, :] = value[:, :, 0:128]
            owns[p][8 * i : 8 * i + 8, 32:64, :] = value[:, :, 128:256]

    def piece_chain(p):
        if p == 0:
            send = lambda way, step: send_a.at[way, step]
            recv = lambda way, step: recv_a.at[way, step]
        else:
            send = lambda way, step: send_bcd.at[p - 1, way, step]
            recv = lambda way, step: recv_bcd.at[p - 1, way, step]
        return reduce_chain(
            p, NY, y, lambda dest: owns[p][pl.ds(dest * NZL, NZL)], send, recv, y_side
        )

    last = [None] * PIECES
    spreads = [[] for _ in range(PIECES)]

    def zl_stage(p, arrived):
        def value(where):
            return (
                owns[p][y * NZL + where]
                + arrived[0][where].astype(F32)
                + arrived[1][where].astype(F32)
            )

        for o in range(1, NZL):
            out = zl_send_a.at[o - 1] if p == 0 else zl_send.at[p - 1, o - 1]
            into = zl_recv_a.at[o - 1] if p == 0 else zl_recv.at[p - 1, o - 1]
            out[...] = value(lax.rem(zl + o, NZL)).astype(BF16)
            spreads[p].append((links.copy(out, into, zl_peer[o - 1]), into))
        last[p] = value(zl)

    def finish(p):
        total = last[p]
        for copy, into in spreads[p]:
            copy.wait_recv()
            total = total + into[...].astype(F32)
        if p < 2:
            out = (expand_ref, reduce_ref)[p]
            out[:, 0:128] = total[0:32, :]
            out[:, 128:256] = total[32:64, :]
            if p == 0:
                line = total[64:65, :]
                picked = line[:, 0:32]
                for k in range(1, NZL):
                    picked = jnp.where(zl == k, line[:, 32 * k : 32 * k + 32], picked)
                gbias_ref[...] = picked
        else:
            for t in range(TPP):
                gtables_ref[(p - 2) * TPP + t] = total[16 * t : 16 * t + 16, :]

    for copy in handed[0]:
        copy.wait_recv()
    for t in range(TABLES):
        own_a[NZL * t : NZL * t + NZL, 64:80, :] = jnp.broadcast_to(
            biases[t : t + 1, :].reshape(1, 1, EMB), (NZL, 16, EMB)
        )
    weight_piece(0, gb_t, low[0])
    chains = [piece_chain(p) for p in range(PIECES)]
    next(chains[0])

    for copy in handed[1]:
        copy.wait_recv()
    weight_piece(1, pooled_t, low[1])
    next(chains[1])
    next(chains[0])

    def cross(i):
        pair = slice(256 * i, 256 * i + 256)
        for c in range(GROUP // 256):
            rows = slice(256 * c, 256 * c + 256)
            inner2 = dot(low[0, rows, :], ew_ref[pair, :], ((1,), (1,)))
            back2 = dot(low[1, rows, :], rw_ref[pair, :], ((1,), (1,)))
            for u in range(2):
                t = 2 * i + u
                columns = slice(t * EMB, (t + 1) * EMB)
                inner = inner2[:, u * EMB : (u + 1) * EMB] + bias_ref[t : t + 1, :]
                xf = pooled[rows, columns].astype(F32)
                crossed_ref[rows, columns] = (xf * inner + xf).astype(BF16)
                gf = cot_ref[rows, columns].astype(F32)
                grad = gf * (inner + 1.0) + back2[:, u * EMB : (u + 1) * EMB]
                spread[rows, columns] = (grad * inv_col[rows, t : t + 1]).astype(BF16)

    def table_piece(p):
        for k in range(TPP):
            t = (p - 2) * TPP + k
            value = dot(counts[t], spread[:, t * EMB : (t + 1) * EMB], ((1,), (0,)))
            owns[p][:, 16 * k : 16 * k + 16, :] = value.reshape(NREP, 16, EMB)

    cross(0)
    cross(1)
    next(chains[1])
    next(chains[0])
    table_piece(2)
    next(chains[2])
    next(chains[1])
    next(chains[0])
    cross(2)
    cross(3)
    next(chains[2])
    next(chains[1])
    table_piece(3)
    next(chains[3])
    next(chains[2])
    zl_stage(0, next(chains[0]))
    next(chains[3])
    next(chains[2])
    zl_stage(1, next(chains[1]))
    next(chains[3])
    finish(0)
    zl_stage(2, next(chains[2]))
    next(chains[3])
    finish(1)
    zl_stage(3, next(chains[3]))
    finish(2)
    finish(3)
    for copy in links.sent:
        copy.wait_send()


def body(tables, feature_ids, bag_lengths, reduce_weight, expand_weight, cross_bias, cotangent):
    vmem = pl.BlockSpec(memory_space=pltpu.VMEM)
    crossed, grad_reduce, grad_expand, grad_bias, grad_tables = pl.pallas_call(
        kernel,
        out_shape=(
            jax.ShapeDtypeStruct((GROUP, FEATURES), BF16),
            jax.ShapeDtypeStruct((FEATURES // NREP, RANK), F32),
            jax.ShapeDtypeStruct((FEATURES // NREP, RANK), F32),
            jax.ShapeDtypeStruct((1, FEATURES // NREP), F32),
            jax.ShapeDtypeStruct((TABLES, ROWS // NREP, EMB), F32),
        ),
        in_specs=[vmem] * 7,
        out_specs=(vmem,) * 5,
        scratch_shapes=[
            pltpu.VMEM((TABLES, ROWS, GROUP), BF16),
            pltpu.VMEM((TABLES, EMB, ROWS), BF16),
            pltpu.VMEM((GROUP, FEATURES), BF16),
            pltpu.VMEM((FEATURES, GROUP), BF16),
            pltpu.VMEM((GROUP, FEATURES), BF16),
            pltpu.VMEM((FEATURES, GROUP), BF16),
            pltpu.VMEM((GROUP, FEATURES), BF16),
            pltpu.VMEM((GROUP, TABLES), F32),
            pltpu.VMEM((TABLES, GROUP), F32),
            pltpu.VMEM((TABLES, EMB), F32),
            pltpu.VMEM((2, HALF, RANK), F32),
            pltpu.VMEM((2, HALF, RANK), F32),
            pltpu.VMEM((2, NX, CHUNK, RANK), F32),
            pltpu.VMEM((2, 2, NX // 2, CHUNK, RANK), BF16),
            pltpu.VMEM((2, 2, NX // 2, CHUNK, RANK), BF16),
            pltpu.VMEM((2, CHUNK, RANK), BF16),
            pltpu.VMEM((2, CHUNK, RANK), BF16),
            pltpu.VMEM((2, GROUP, RANK), BF16),
            pltpu.VMEM((NREP, TALL, EMB), F32),
            pltpu.VMEM((NREP, WIDE, EMB), F32),
            pltpu.VMEM((NREP, WIDE, EMB), F32),
            pltpu.VMEM((NREP, WIDE, EMB), F32),
            pltpu.VMEM((2, NY // 2, NZL, TALL, EMB), BF16),
            pltpu.VMEM((PIECES - 1, 2, NY // 2, NZL, WIDE, EMB), BF16),
            pltpu.VMEM((2, NY // 2, NZL, TALL, EMB), BF16),
            pltpu.VMEM((PIECES - 1, 2, NY // 2, NZL, WIDE, EMB), BF16),
            pltpu.VMEM((NZL - 1, TALL, EMB), BF16),
            pltpu.VMEM((PIECES - 1, NZL - 1, WIDE, EMB), BF16),
            pltpu.VMEM((NZL - 1, TALL, EMB), BF16),
            pltpu.VMEM((PIECES - 1, NZL - 1, WIDE, EMB), BF16),
            pltpu.SemaphoreType.DMA((COPIES,)),
            pltpu.SemaphoreType.DMA((COPIES,)),
        ],
        compiler_params=pltpu.CompilerParams(
            collective_id=0, has_side_effects=True, vmem_limit_bytes=56 << 20
        ),
        cost_estimate=pl.CostEstimate(
            flops=5 << 30, bytes_accessed=8 << 20, transcendentals=0
        ),
    )(
        jnp.transpose(feature_ids, (1, 2, 0)),
        bag_lengths.T,
        tables,
        reduce_weight,
        expand_weight,
        cross_bias.reshape(TABLES, EMB),
        cotangent,
    )
    return crossed, grad_reduce, grad_expand, grad_bias.reshape(-1), grad_tables


def solution(mesh):
    in_specs = (
        P("mp", None, None),
        P("replica", "mp", None),
        P("replica", "mp"),
        P("mp", None),
        P("mp", None),
        P("mp"),
        P("replica", "mp"),
    )
    out_specs = (
        P("replica", "mp"),
        P(("mp", "replica"), None),
        P(("mp", "replica"), None),
        P(("mp", "replica")),
        P("mp", "replica", None),
    )
    return jax.shard_map(body, mesh=mesh, in_specs=in_specs, out_specs=out_specs, check_vma=False)
```

time: 769 us -> 108 us (0.14)
  waiting for transfers between devices: 365 us -> 0 us
  blocking collectives: 266 us -> 0 us
  Pallas kernels: 0 us -> 102 us
  matrix products: 65.5 us -> 0 us
  other arithmetic: 27.8 us -> 0 us
  local copies, waits for them, and re-layouts: 27.4 us -> 5.09 us
  between operations: 14.5 us -> 0.68 us
    reduce_scatter x3 -> x0, waiting for transfers between devices: 365 us -> none  [the longest x1 169 us: body(): lax.psum_scatter(part_tables, 'replica', scatter_dimension=1, tiled=True)]
    psum x1 -> x0, blocking collectives: 183 us -> none  [rank_total(): return lax.psum(partial_value, 'mp').astype(jnp.bfloat16)]
    pallas_call x0 -> x1, Pallas kernels: none -> 102 us  [body(): pl.pallas_call(kernel, out_shape=(jax.ShapeDtypeStruct((GROUP, FEATURES),...]
    unnamed x1 -> x0, blocking collectives: 82.8 us -> none
    dot_general x22 -> x0, matrix products: 65.5 us -> none  [the longest x8 35.8 us: spread_table(): jnp.dot(counts.T, scaled, preferred_element_type=jnp.float32, precision=l...]
    reduce_sum x16 -> x0, other arithmetic: 27.6 us -> none  [bag_counts(): jnp.sum(jnp.where(match & live[:, :, None], jnp.float32(1.0), jnp.float32...]
    dynamic_slice x16 -> x0, local copies, waits for them, and re-layouts: 12.2 us -> none  [body(): lax.map(lambda a: pool_table(a[0], a[1], a[2]), (tables, ids_t, lens_t))]
    eq x16 -> x0, local copies, waits for them, and re-layouts: 11.4 us -> none  [bag_counts(): id_cols[:, :, None] == jnp.arange(row_count, dtype=jnp.int32)[None, None, :]]
  transfers between devices with their start and end apart: 3 -> 0, of which waited for: 3 -> 0; matrix products, arithmetic and copies ran while one was open for 9% -> 0% of each run, Pallas kernels for 0% -> 0%
where the time goes in v1:
time: 108 us
  Pallas kernels  102 us (94%)
  local copies, waits for them, and re-layouts  5.09 us (5%)
    pallas_call x1, Pallas kernels, body(): pl.pallas_call(kernel, out_shape=(jax.ShapeDtypeStruct((GROUP, FEATURES),...  102 us
    unnamed x13, local copies, waits for them, and re-layouts  5.09 us

profile of v1, /device:TPU:4, one launch (start us, length us, event | category | flops | bytes accessed | tf_op | source)
XLA Modules:
  0.0 107.9 jit_solution(8191583604713759914)
XLA Ops:
  0.6 102.1 %shard_map.110 = (bf16[768,1024]{1,0:T(8,128)(2,1)}, f32[32,256]{1,0:T(8,128)}, f32[32,256]{1,0:T(8,128)}, f32[1,32]{1,0:T(1,128)}, f32[8,16,128]{2,1,0:T(8,128)}) custom-call(s32[8,4,768]{2,1,0:T(4,128)} %bitcast.4, s32[8,768]{1,0:T(8,128)} %bitcast.5, bf16[8,512,128]{2,1,0:T(8,128)(2,1)} %tables_ref.1, bf16[1024,256]{1,0:T(8,128)(2,1)} %rw_ref.1, ...), custom_call_target="tpu_custom_call" | custom-call | flops 5368709120 | bytes 8388608 | tf_op jit(solution)/shard_map/pallas_call | solution.py:345
  102.8 0.0 copy-start.2
  102.8 0.0 copy-start.1
  102.8 0.0 copy-start.3
  102.8 0.0 copy-start
  102.8 2.7 %copy.17 = bf16[768,1024]{1,0:T(8,128)(2,1)} copy(bf16[768,1024]{1,0:T(8,128)(2,1)} %get-tuple-element.20) | data formatting | bytes 3145728
  105.5 0.0 copy-done.2
  105.5 0.6 copy.18
  106.1 0.0 copy-done.1
  106.1 0.6 copy.19
  106.8 0.0 copy-done.3
  106.8 0.5 copy.20
  107.3 0.0 copy-done
  107.3 0.6 copy.21
Async XLA Ops:
  102.8 2.7 %copy-start.2 = (f32[32,256]{1,0:T(8,128)S(1)}, f32[32,256]{1,0:T(8,128)}, u32[]{:S(2)}) copy-start(f32[32,256]{1,0:T(8,128)} %get-tuple-element.21) | copy-start | bytes 98308
  102.8 3.4 %copy-start.1 = (f32[32,256]{1,0:T(8,128)S(1)}, f32[32,256]{1,0:T(8,128)}, u32[]{:S(2)}) copy-start(f32[32,256]{1,0:T(8,128)} %get-tuple-element.22) | copy-start | bytes 98308
  102.8 4.0 %copy-start.3 = (f32[1,32]{1,0:T(1,128)S(1)}, f32[1,32]{1,0:T(1,128)}, u32[]{:S(2)}) copy-start(f32[1,32]{1,0:T(1,128)} %get-tuple-element.13) | copy-start | bytes 388
  102.8 4.5 %copy-start = (f32[8,16,128]{2,1,0:T(8,128)S(1)}, f32[8,16,128]{2,1,0:T(8,128)}, u32[]{:S(2)}) copy-start(f32[8,16,128]{2,1,0:T(8,128)} %get-tuple-element.24) | copy-start | bytes 196612

commit v2 on v1

--- a/solution.py
+++ b/solution.py
@@ -17,6 +17,7 @@
 TPP = 4
 WIDE = 64
 TALL = 80
+FAR_FIRST = (4, 3, 5, 2, 6, 1, 7)
 MESH = pl.DeviceIdType.MESH
 BF16 = jnp.bfloat16
 F32 = jnp.float32
@@ -57,11 +58,13 @@
 
 
 def kernel(
-    ids_ref, lens_ref, tables_ref, rw_ref, ew_ref, bias_ref, cot_ref,
+    ids_hbm, lens_hbm, tables_hbm, cot_hbm, rw_hbm, ew_hbm, bias_hbm,
     crossed_ref, reduce_ref, expand_ref, gbias_ref, gtables_ref,
+    ids_ref, lens_ref, tables_ref, cot_ref, rw_ref, ew_ref, bias_ref, load_sems,
     counts, tabs_t, pooled, pooled_t, gb, gb_t, spread, inv_col, inv_row, biases,
     core_send, core_recv, rank_own, rank_send, rank_recv, zh_send, zh_recv, low,
-    own_a, own_b, own_c, own_d, send_a, send_bcd, recv_a, recv_bcd, zl_send_a, zl_send, zl_recv_a, zl_recv,
+    own_a, own_b, own_c, own_d, near_send, near_recv, across_send, across_recv,
+    send_a, send_bcd, recv_a, recv_bcd, zl_send, zl_recv,
     send_sems, recv_sems,
 ):
     m, r = lax.axis_index("mp"), lax.axis_index("replica")
@@ -80,48 +83,58 @@
     zl_peer = [rep_at(y, lax.rem(zl + o, NZL)) for o in range(1, NZL)]
 
     barrier = pltpu.get_barrier_semaphore()
-    greeted = [*x_side, *y_side, other_core, other_zh, *zl_peer]
+    x_peer = [mp_at(lax.rem(x + o, NX), zh, core) for o in range(1, NX)]
+    greeted = [*x_peer, *y_side, other_core, other_zh, *zl_peer]
     for device in greeted:
         pl.semaphore_signal(barrier, inc=1, device_id=device, device_id_type=MESH)
 
+    inputs = (ids_hbm, lens_hbm, tables_hbm, cot_hbm, rw_hbm, ew_hbm, bias_hbm)
+    places = (ids_ref, lens_ref, tables_ref, cot_ref, rw_ref, ew_ref, bias_ref)
+    loads = []
+    for i in range(len(inputs)):
+        loads.append(pltpu.make_async_copy(inputs[i], places[i], load_sems.at[i]))
+        loads[i].start()
+
     links = Links(send_sems, recv_sems)
 
+    loads[0].wait()
+    loads[1].wait()
     inv_row[...] = 1.0 / lens_ref[...].astype(F32)
     inv_col[...] = jnp.transpose(inv_row[...])
     biases[...] = jnp.zeros_like(biases)
 
-    def make_tab(t, carry):
-        tabs_t[t] = jnp.transpose(tables_ref[t])
-        return carry
-
-    lax.fori_loop(0, TABLES, make_tab, 0)
-
-    def half(start):
+    def half(start, first):
         span = pl.ds(pl.multiple_of(start, 128), HALF)
-        row_of = lax.broadcasted_iota(jnp.int32, (64, HALF), 0)
-
-        def table(t, carry):
-            lens = lens_ref[pl.ds(t, 1), span]
+        row_of = lax.broadcasted_iota(jnp.int32, (64, HALF), 0).astype(F32).astype(BF16)
+        one, zero = jnp.ones((), BF16), jnp.zeros((64, HALF), BF16)
+        for t in range(TABLES):
+            lens = lens_ref[t : t + 1, span]
             picks = []
             for j in range(HOT):
                 picks.append(jnp.where(lens > j, ids_ref[t, j : j + 1, span], -1))
             for c in range(ROWS // 64):
-                total = jnp.zeros((64, HALF), F32)
+                total = zero
                 for j in range(HOT):
-                    total = jnp.where(row_of == picks[j] - 64 * c, total + 1.0, total)
-                counts[t, 64 * c : 64 * c + 64, span] = total.astype(BF16)
-            columns = pl.ds(pl.multiple_of(t * EMB, EMB), EMB)
+                    pick = (picks[j] - 64 * c).astype(F32).astype(BF16)
+                    total = jnp.where(row_of == pick, total + one, total)
+                counts[t, 64 * c : 64 * c + 64, span] = total
+            if first:
+                if t == 0:
+                    loads[2].wait()
+                    loads[3].wait()
+                tabs_t[t] = jnp.transpose(tables_ref[t])
+            columns = slice(t * EMB, (t + 1) * EMB)
             sums = dot(tabs_t[t], counts[t, :, span], ((1,), (0,)))
-            mean_t = (sums * inv_row[pl.ds(t, 1), span]).astype(BF16)
+            mean_t = (sums * inv_row[t : t + 1, span]).astype(BF16)
             pooled_t[columns, span] = mean_t
             mean = jnp.transpose(mean_t)
             pooled[pl.ds(start, HALF), columns] = mean
             grad = cot_ref[pl.ds(start, HALF), columns].astype(F32) * mean.astype(F32)
             gb[pl.ds(start, HALF), columns] = grad.astype(BF16)
-            biases[pl.ds(t, 1), :] += jnp.sum(grad, axis=0, keepdims=True)
-            return carry
-
-        lax.fori_loop(0, TABLES, table, 0)
+            biases[t : t + 1, :] += jnp.sum(grad, axis=0, keepdims=True)
+        if first:
+            for i in range(4, 7):
+                loads[i].wait()
         rows = pl.ds(start, HALF)
         return (
             dot(pooled[rows, :], rw_ref[...], ((1,), (0,))),
@@ -130,12 +143,12 @@
 
     theirs = pl.multiple_of((1 - core) * HALF, HALF)
     mine = pl.multiple_of(core * HALF, HALF)
-    parts = half(theirs)
+    parts = half(theirs, True)
     core_send[0] = parts[0]
     core_send[1] = parts[1]
     pl.semaphore_wait(barrier, len(greeted))
     from_core = links.copy(core_send, core_recv, other_core)
-    parts = half(mine)
+    parts = half(mine, False)
     from_core.wait_recv()
     for p in range(2):
         rank_own[p] = (parts[p] + core_recv[p]).reshape(NX, CHUNK, RANK)
@@ -160,31 +173,24 @@
             flights[way][-1].wait_recv()
         yield [recv(way, count[way] - 1) for way in range(2)]
 
-    rank_chains = [
-        reduce_chain(
-            p, NX, x,
-            lambda dest, p=p: rank_own[p, dest],
-            lambda way, step, p=p: rank_send.at[p, way, step],
-            lambda way, step, p=p: rank_recv.at[p, way, step],
-            x_side,
-        )
-        for p in range(2)
-    ]
-
-    def flip(t):
+    scatters = [[], []]
+    for p in range(2):
+        for o in FAR_FIRST:
+            rank_send[p, o - 1] = rank_own[p, lax.rem(x + o, NX)].astype(BF16)
+            scatters[p].append(
+                links.copy(rank_send.at[p, o - 1], rank_recv.at[p, o - 1], x_peer[o - 1])
+            )
+
+    for t in range(TABLES):
         gb_t[t * EMB : (t + 1) * EMB, :] = jnp.transpose(gb[:, t * EMB : (t + 1) * EMB])
-
-    for step in range(NX // 2):
-        for p in range(2):
-            next(rank_chains[p])
-        flip(2 * step)
-        flip(2 * step + 1)
 
     summed = []
     swaps = []
     for p in range(2):
-        arrived = next(rank_chains[p])
-        value = rank_own[p, x] + arrived[0][...].astype(F32) + arrived[1][...].astype(F32)
+        value = rank_own[p, x]
+        for i, o in enumerate(FAR_FIRST):
+            scatters[p][i].wait_recv()
+            value = value + rank_recv[p, o - 1].astype(F32)
         summed.append(value)
         zh_send[p] = value.astype(BF16)
         swaps.append(links.copy(zh_send.at[p], zh_recv.at[p], other_zh))
@@ -193,26 +199,17 @@
         return low.at[p, pl.ds(pl.multiple_of(mine + xx * CHUNK, 16), CHUNK), :]
 
     handed = [[], []]
-    gathers = [[[], []], [[], []]]
+    gathers = [[], []]
     for p in range(2):
         swaps[p].wait_recv()
         block(p, x)[...] = (summed[p] + zh_recv[p].astype(F32)).astype(BF16)
-        for way in range(2):
-            gathers[p][way].append(links.copy(block(p, x), block(p, x), x_side[way]))
-        handed[p].append(links.copy(block(p, x), block(p, x), other_core))
-    for step in range(1, NX // 2 + 1):
-        for p in range(2):
-            for way in range(2):
-                count = hops(p, way, NX)
-                if step > count:
-                    continue
-                source = lax.rem(x + NX - step, NX) if way == 0 else lax.rem(x + step, NX)
-                gathers[p][way][step - 1].wait_recv()
-                if step < count:
-                    gathers[p][way].append(
-                        links.copy(block(p, source), block(p, source), x_side[way])
-                    )
-                handed[p].append(links.copy(block(p, source), block(p, source), other_core))
+        for o in FAR_FIRST:
+            gathers[p].append(links.copy(block(p, x), block(p, x), x_peer[o - 1]))
+    for p in range(2):
+        for copy in gathers[p]:
+            copy.wait_recv()
+        rows = low.at[p, pl.ds(mine, HALF), :]
+        handed[p].append(links.copy(rows, rows, other_core))
 
     owns = [own_a, own_b, own_c, own_d]
 
@@ -220,18 +217,45 @@
         for i in range(TABLES // 2):
             value = dot(left[256 * i : 256 * i + 256, :], right, ((1,), (0,)))
             value = value.reshape(8, 32, RANK)
+            if p == 0:
+                for k in range(8):
+                    own_a[k % NZL, 2 * i + k // NZL, 0:32, :] = value[k, :, 0:128]
+                    own_a[k % NZL, 2 * i + k // NZL, 32:64, :] = value[k, :, 128:256]
+                continue
             owns[p][8 * i : 8 * i + 8, 0:32, :] = value[:, :, 0:128]
             owns[p][8 * i : 8 * i + 8, 32:64, :] = value[:, :, 128:256]
 
     def piece_chain(p):
-        if p == 0:
-            send = lambda way, step: send_a.at[way, step]
-            recv = lambda way, step: recv_a.at[way, step]
-        else:
-            send = lambda way, step: send_bcd.at[p - 1, way, step]
-            recv = lambda way, step: recv_bcd.at[p - 1, way, step]
         return reduce_chain(
-            p, NY, y, lambda dest: owns[p][pl.ds(dest * NZL, NZL)], send, recv, y_side
+            p, NY, y,
+            lambda dest: owns[p][pl.ds(dest * NZL, NZL)],
+            lambda way, step: send_bcd.at[p - 1, way, step],
+            lambda way, step: recv_bcd.at[p - 1, way, step],
+            y_side,
+        )
+
+    def first_chain():
+        near = zl + 1 - 2 * lax.rem(zl, 2)
+        across = lax.rem(zl + 2, NZL)
+        firsts = []
+        for k, keeper in enumerate((lax.rem(near + 2, NZL), near)):
+            near_send[k] = own_a[keeper].astype(BF16)
+            firsts.append(links.copy(near_send.at[k], near_recv.at[k], rep_at(y, near)))
+        yield
+        firsts[0].wait_recv()
+        across_send[...] = (own_a[across] + near_recv[0].astype(F32)).astype(BF16)
+        second = links.copy(across_send, across_recv, rep_at(y, across))
+        yield
+        firsts[1].wait_recv()
+        second.wait_recv()
+        for k in range(NY):
+            own_a[zl, k] += near_recv[1, k].astype(F32) + across_recv[k].astype(F32)
+        yield from reduce_chain(
+            0, NY, y,
+            lambda dest: own_a[zl, dest],
+            lambda way, step: send_a.at[way, step],
+            lambda way, step: recv_a.at[way, step],
+            y_side,
         )
 
     last = [None] * PIECES
@@ -246,8 +270,7 @@
             )
 
         for o in range(1, NZL):
-            out = zl_send_a.at[o - 1] if p == 0 else zl_send.at[p - 1, o - 1]
-            into = zl_recv_a.at[o - 1] if p == 0 else zl_recv.at[p - 1, o - 1]
+            out, into = zl_send.at[p - 1, o - 1], zl_recv.at[p - 1, o - 1]
             out[...] = value(lax.rem(zl + o, NZL)).astype(BF16)
             spreads[p].append((links.copy(out, into, zl_peer[o - 1]), into))
         last[p] = value(zl)
@@ -274,18 +297,17 @@
     for copy in handed[0]:
         copy.wait_recv()
     for t in range(TABLES):
-        own_a[NZL * t : NZL * t + NZL, 64:80, :] = jnp.broadcast_to(
+        own_a[:, t, 64:80, :] = jnp.broadcast_to(
             biases[t : t + 1, :].reshape(1, 1, EMB), (NZL, 16, EMB)
         )
     weight_piece(0, gb_t, low[0])
-    chains = [piece_chain(p) for p in range(PIECES)]
+    chains = [first_chain()] + [piece_chain(p) for p in range(1, PIECES)]
     next(chains[0])
 
     for copy in handed[1]:
         copy.wait_recv()
     weight_piece(1, pooled_t, low[1])
     next(chains[1])
-    next(chains[0])
 
     def cross(i):
         pair = slice(256 * i, 256 * i + 256)
@@ -312,7 +334,6 @@
     cross(0)
     cross(1)
     next(chains[1])
-    next(chains[0])
     table_piece(2)
     next(chains[2])
     next(chains[1])
@@ -324,36 +345,60 @@
     table_piece(3)
     next(chains[3])
     next(chains[2])
-    zl_stage(0, next(chains[0]))
+    next(chains[0])
     next(chains[3])
+    zl_stage(1, next(chains[1]))
     next(chains[2])
-    zl_stage(1, next(chains[1]))
+    next(chains[0])
     next(chains[3])
-    finish(0)
     zl_stage(2, next(chains[2]))
+    next(chains[0])
     next(chains[3])
     finish(1)
+    next(chains[0])
     zl_stage(3, next(chains[3]))
+    arrived = next(chains[0])
+    last[0] = own_a[zl, y] + arrived[0][...].astype(F32) + arrived[1][...].astype(F32)
+    finish(0)
     finish(2)
     finish(3)
     for copy in links.sent:
         copy.wait_send()
 
 
+def hand_out(*refs):
+    sems = refs[10]
+    copies = [pltpu.make_async_copy(refs[i], refs[5 + i], sems.at[i]) for i in range(5)]
+    for copy in copies:
+        copy.start()
+    for copy in copies:
+        copy.wait()
+
+
 def body(tables, feature_ids, bag_lengths, reduce_weight, expand_weight, cross_bias, cotangent):
     vmem = pl.BlockSpec(memory_space=pltpu.VMEM)
-    crossed, grad_reduce, grad_expand, grad_bias, grad_tables = pl.pallas_call(
+    anywhere = pl.BlockSpec(memory_space=pl.ANY)
+    kept = (
+        ((GROUP, FEATURES), BF16),
+        ((FEATURES // NREP, RANK), F32),
+        ((FEATURES // NREP, RANK), F32),
+        ((1, FEATURES // NREP), F32),
+        ((TABLES, ROWS // NREP, EMB), F32),
+    )
+    made = pl.pallas_call(
         kernel,
-        out_shape=(
-            jax.ShapeDtypeStruct((GROUP, FEATURES), BF16),
-            jax.ShapeDtypeStruct((FEATURES // NREP, RANK), F32),
-            jax.ShapeDtypeStruct((FEATURES // NREP, RANK), F32),
-            jax.ShapeDtypeStruct((1, FEATURES // NREP), F32),
-            jax.ShapeDtypeStruct((TABLES, ROWS // NREP, EMB), F32),
-        ),
-        in_specs=[vmem] * 7,
+        out_shape=tuple(pltpu.VMEM(*k) for k in kept),
+        in_specs=[pl.BlockSpec(memory_space=pltpu.HBM)] * 7,
         out_specs=(vmem,) * 5,
         scratch_shapes=[
+            pltpu.VMEM((TABLES, HOT, GROUP), jnp.int32),
+            pltpu.VMEM((TABLES, GROUP), jnp.int32),
+            pltpu.VMEM((TABLES, ROWS, EMB), BF16),
+            pltpu.VMEM((GROUP, FEATURES), BF16),
+            pltpu.VMEM((FEATURES, RANK), BF16),
+            pltpu.VMEM((FEATURES, RANK), BF16),
+            pltpu.VMEM((TABLES, EMB), F32),
+            pltpu.SemaphoreType.DMA((7,)),
             pltpu.VMEM((TABLES, ROWS, GROUP), BF16),
             pltpu.VMEM((TABLES, EMB, ROWS), BF16),
             pltpu.VMEM((GROUP, FEATURES), BF16),
@@ -367,28 +412,30 @@
             pltpu.VMEM((2, HALF, RANK), F32),
             pltpu.VMEM((2, HALF, RANK), F32),
             pltpu.VMEM((2, NX, CHUNK, RANK), F32),
-            pltpu.VMEM((2, 2, NX // 2, CHUNK, RANK), BF16),
-            pltpu.VMEM((2, 2, NX // 2, CHUNK, RANK), BF16),
+            pltpu.VMEM((2, NX - 1, CHUNK, RANK), BF16),
+            pltpu.VMEM((2, NX - 1, CHUNK, RANK), BF16),
             pltpu.VMEM((2, CHUNK, RANK), BF16),
             pltpu.VMEM((2, CHUNK, RANK), BF16),
             pltpu.VMEM((2, GROUP, RANK), BF16),
-            pltpu.VMEM((NREP, TALL, EMB), F32),
+            pltpu.VMEM((NZL, NY, TALL, EMB), F32),
             pltpu.VMEM((NREP, WIDE, EMB), F32),
             pltpu.VMEM((NREP, WIDE, EMB), F32),
             pltpu.VMEM((NREP, WIDE, EMB), F32),
-            pltpu.VMEM((2, NY // 2, NZL, TALL, EMB), BF16),
+            pltpu.VMEM((2, NY, TALL, EMB), BF16),
+            pltpu.VMEM((2, NY, TALL, EMB), BF16),
+            pltpu.VMEM((NY, TALL, EMB), BF16),
+            pltpu.VMEM((NY, TALL, EMB), BF16),
+            pltpu.VMEM((2, NY // 2, TALL, EMB), BF16),
             pltpu.VMEM((PIECES - 1, 2, NY // 2, NZL, WIDE, EMB), BF16),
-            pltpu.VMEM((2, NY // 2, NZL, TALL, EMB), BF16),
+            pltpu.VMEM((2, NY // 2, TALL, EMB), BF16),
             pltpu.VMEM((PIECES - 1, 2, NY // 2, NZL, WIDE, EMB), BF16),
-            pltpu.VMEM((NZL - 1, TALL, EMB), BF16),
             pltpu.VMEM((PIECES - 1, NZL - 1, WIDE, EMB), BF16),
-            pltpu.VMEM((NZL - 1, TALL, EMB), BF16),
             pltpu.VMEM((PIECES - 1, NZL - 1, WIDE, EMB), BF16),
             pltpu.SemaphoreType.DMA((COPIES,)),
             pltpu.SemaphoreType.DMA((COPIES,)),
         ],
         compiler_params=pltpu.CompilerParams(
-            collective_id=0, has_side_effects=True, vmem_limit_bytes=56 << 20
+            collective_id=0, has_side_effects=True, vmem_limit_bytes=62 << 20
         ),
         cost_estimate=pl.CostEstimate(
             flops=5 << 30, bytes_accessed=8 << 20, transcendentals=0
@@ -397,11 +444,12 @@
         jnp.transpose(feature_ids, (1, 2, 0)),
         bag_lengths.T,
         tables,
+        cotangent,
         reduce_weight,
         expand_weight,
         cross_bias.reshape(TABLES, EMB),
-        cotangent,
     )
+    crossed, grad_reduce, grad_expand, grad_bias, grad_tables = made
     return crossed, grad_reduce, grad_expand, grad_bias.reshape(-1), grad_tables
 
 

time: 108 us -> 88.6 us (0.82)
  the two profiles are of different devices: /device:TPU:4 before, /device:TPU:2 now
where the time goes in v2:
time: 88.6 us; the launch traced here: 88.4 us
  Pallas kernels  84.3 us (95%)
  local copies, waits for them, and re-layouts  3.51 us (4%)
    pallas_call x1, Pallas kernels, body(): pl.pallas_call(kernel, out_shape=tuple((pltpu.VMEM(*k) for k in kept)), i...  84.3 us
    unnamed x5, local copies, waits for them, and re-layouts  3.51 us

profile of v2, /device:TPU:2, one launch (start us, length us, event | category | flops | bytes accessed | tf_op | source)
XLA Modules:
  0.0 88.4 jit_solution(12617382065871321745)
XLA Ops:
  0.6 84.3 %shard_map.110 = (bf16[768,1024]{1,0:T(8,128)(2,1)S(1)}, f32[32,256]{1,0:T(8,128)S(1)}, f32[32,256]{1,0:T(8,128)S(1)}, f32[1,32]{1,0:T(1,128)S(1)}, f32[8,16,128]{2,1,0:T(8,128)S(1)}) custom-call(s32[8,4,768]{2,1,0:T(4,128)} %bitcast.5, s32[8,768]{1,0:T(8,128)} %bitcast.6, bf16[8,512,128]{2,1,0:T(8,128)(2,1)} %tables_hbm.1, bf16[768,1024]{1,0:T(8,128)(2,1)} %cot_hbm.1, ...), custom_call_target="tpu_custom_call" | custom-call | flops 5368709120 | bytes 8388608 | tf_op jit(solution)/shard_map/pallas_call | solution.py:388
  84.9 1.1 %copy.17 = bf16[768,1024]{1,0:T(8,128)(2,1)} copy(bf16[768,1024]{1,0:T(8,128)(2,1)S(1)} %get-tuple-element.15) | data formatting | bytes 3145728
  86.1 0.5 copy.20
  86.6 0.6 copy.18
  87.2 0.6 copy.19
  87.8 0.6 copy.21

commit v3 on v2

--- a/solution.py
+++ b/solution.py
@@ -17,7 +17,6 @@
 TPP = 4
 WIDE = 64
 TALL = 80
-FAR_FIRST = (4, 3, 5, 2, 6, 1, 7)
 MESH = pl.DeviceIdType.MESH
 BF16 = jnp.bfloat16
 F32 = jnp.float32
@@ -54,7 +53,7 @@
         return made
 
 
-COPIES = 1 + 14 + 2 + 14 + 16 + 7 * PIECES + 3 * PIECES
+COPIES = 2 + 14 + 2 + 14 + 2 + 3 + 7 * PIECES + 3 * (PIECES - 1)
 
 
 def kernel(
@@ -77,14 +76,18 @@
     def rep_at(yy, zz):
         return {"replica": yy * NZL + zz}
 
-    x_side = (mp_at(lax.rem(x + 1, NX), zh, core), mp_at(lax.rem(x + NX - 1, NX), zh, core))
     y_side = (rep_at(lax.rem(y + 1, NY), zl), rep_at(lax.rem(y + NY - 1, NY), zl))
     other_core, other_zh = mp_at(x, zh, 1 - core), mp_at(x, 1 - zh, core)
     zl_peer = [rep_at(y, lax.rem(zl + o, NZL)) for o in range(1, NZL)]
 
+    x_at = [
+        [x] + [lax.rem(x + o, NX) for o in range(1, 5)],
+        [x] + [lax.rem(x + NX - o, NX) for o in range(1, 5)],
+    ]
+    x_dev = [[None] + [mp_at(x_at[way][o], zh, core) for o in (1, 2)] for way in range(2)]
+
     barrier = pltpu.get_barrier_semaphore()
-    x_peer = [mp_at(lax.rem(x + o, NX), zh, core) for o in range(1, NX)]
-    greeted = [*x_peer, *y_side, other_core, other_zh, *zl_peer]
+    greeted = [*x_dev[0][1:], *x_dev[1][1:], *y_side, other_core, other_zh, *zl_peer]
     for device in greeted:
         pl.semaphore_signal(barrier, inc=1, device_id=device, device_id_type=MESH)
 
@@ -144,14 +147,100 @@
     theirs = pl.multiple_of((1 - core) * HALF, HALF)
     mine = pl.multiple_of(core * HALF, HALF)
     parts = half(theirs, True)
-    core_send[0] = parts[0]
-    core_send[1] = parts[1]
+    for p in range(2):
+        core_send[p] = parts[p].astype(BF16)
     pl.semaphore_wait(barrier, len(greeted))
-    from_core = links.copy(core_send, core_recv, other_core)
+    from_core = [
+        links.copy(core_send.at[p], core_recv.at[p], other_core) for p in range(2)
+    ]
     parts = half(mine, False)
-    from_core.wait_recv()
-    for p in range(2):
-        rank_own[p] = (parts[p] + core_recv[p]).reshape(NX, CHUNK, RANK)
+
+    scatters = [{}, {}]
+    gathers = [{}, {}]
+    swaps = [None, None]
+    summed = [None, None]
+    handed = [None, None]
+
+    def scatter(p, way, d, value, to):
+        rank_send[p, way, d - 1] = value.astype(BF16)
+        scatters[p][way, d] = links.copy(
+            rank_send.at[p, way, d - 1], rank_recv.at[p, way, d - 1], x_dev[way][to]
+        )
+
+    def arrived(p, way, d):
+        scatters[p][way, d].wait_recv()
+        return rank_recv[p, way, d - 1].astype(F32)
+
+    def scatter_first(p):
+        from_core[p].wait_recv()
+        rank_own[p] = (parts[p] + core_recv[p].astype(F32)).reshape(NX, CHUNK, RANK)
+        for way in range(2):
+            if hops(p, way, NX) == 4:
+                scatter(p, way, 4, rank_own[p, x_at[way][4]], 2)
+        for way in range(2):
+            scatter(p, way, 3, rank_own[p, x_at[way][3]], 1)
+        for way in range(2):
+            scatter(p, way, 1, rank_own[p, x_at[way][1]], 1)
+
+    def scatter_second(p):
+        for way in range(2):
+            value = rank_own[p, x_at[way][2]] + arrived(p, way, 3)
+            if hops(p, way, NX) == 4:
+                value = value + arrived(p, way, 4)
+            scatter(p, way, 2, value, 2)
+
+    def scatter_last(p):
+        value = rank_own[p, x]
+        for d in (1, 2):
+            for way in range(2):
+                value = value + arrived(p, way, d)
+        summed[p] = value
+        zh_send[p] = value.astype(BF16)
+        swaps[p] = links.copy(zh_send.at[p], zh_recv.at[p], other_zh)
+
+    def block(p, xx):
+        return low.at[p, pl.ds(pl.multiple_of(mine + xx * CHUNK, 16), CHUNK), :]
+
+    def gather_first(p):
+        swaps[p].wait_recv()
+        block(p, x)[...] = (summed[p] + zh_recv[p].astype(F32)).astype(BF16)
+        for d in (2, 1):
+            for way in range(2):
+                gathers[p][way, d] = links.copy(block(p, x), block(p, x), x_dev[way][d])
+
+    def gather_second(p):
+        for way in range(2):
+            source = block(p, x_at[1 - way][2])
+            gathers[p][way, 2].wait_recv()
+            for d in range(3, hops(p, way, NX) + 1):
+                gathers[p][way, d] = links.copy(source, source, x_dev[way][d - 2])
+
+    def gather_last(p):
+        for (way, d), copy in gathers[p].items():
+            if d != 2:
+                copy.wait_recv()
+        rows = low.at[p, pl.ds(mine, HALF), :]
+        handed[p] = links.copy(rows, rows, other_core)
+
+    def flip(t):
+        gb_t[t * EMB : (t + 1) * EMB, :] = jnp.transpose(gb[:, t * EMB : (t + 1) * EMB])
+
+    scatter_first(0)
+    scatter_first(1)
+    for t in range(TABLES // 2):
+        flip(t)
+    scatter_second(0)
+    scatter_second(1)
+    for t in range(TABLES // 2, TABLES):
+        flip(t)
+    scatter_last(0)
+    scatter_last(1)
+    gather_first(0)
+    gather_first(1)
+    gather_second(0)
+    gather_second(1)
+    gather_last(0)
+    gather_last(1)
 
     def reduce_chain(part, n, me, own, send, recv, sides):
         count = [hops(part, way, n) for way in range(2)]
@@ -172,44 +261,6 @@
         for way in range(2):
             flights[way][-1].wait_recv()
         yield [recv(way, count[way] - 1) for way in range(2)]
-
-    scatters = [[], []]
-    for p in range(2):
-        for o in FAR_FIRST:
-            rank_send[p, o - 1] = rank_own[p, lax.rem(x + o, NX)].astype(BF16)
-            scatters[p].append(
-                links.copy(rank_send.at[p, o - 1], rank_recv.at[p, o - 1], x_peer[o - 1])
-            )
-
-    for t in range(TABLES):
-        gb_t[t * EMB : (t + 1) * EMB, :] = jnp.transpose(gb[:, t * EMB : (t + 1) * EMB])
-
-    summed = []
-    swaps = []
-    for p in range(2):
-        value = rank_own[p, x]
-        for i, o in enumerate(FAR_FIRST):
-            scatters[p][i].wait_recv()
-            value = value + rank_recv[p, o - 1].astype(F32)
-        summed.append(value)
-        zh_send[p] = value.astype(BF16)
-        swaps.append(links.copy(zh_send.at[p], zh_recv.at[p], other_zh))
-
-    def block(p, xx):
-        return low.at[p, pl.ds(pl.multiple_of(mine + xx * CHUNK, 16), CHUNK), :]
-
-    handed = [[], []]
-    gathers = [[], []]
-    for p in range(2):
-        swaps[p].wait_recv()
-        block(p, x)[...] = (summed[p] + zh_recv[p].astype(F32)).astype(BF16)
-        for o in FAR_FIRST:
-            gathers[p].append(links.copy(block(p, x), block(p, x), x_peer[o - 1]))
-    for p in range(2):
-        for copy in gathers[p]:
-            copy.wait_recv()
-        rows = low.at[p, pl.ds(mine, HALF), :]
-        handed[p].append(links.copy(rows, rows, other_core))
 
     owns = [own_a, own_b, own_c, own_d]
 
@@ -294,8 +345,7 @@
             for t in range(TPP):
                 gtables_ref[(p - 2) * TPP + t] = total[16 * t : 16 * t + 16, :]
 
-    for copy in handed[0]:
-        copy.wait_recv()
+    handed[0].wait_recv()
     for t in range(TABLES):
         own_a[:, t, 64:80, :] = jnp.broadcast_to(
             biases[t : t + 1, :].reshape(1, 1, EMB), (NZL, 16, EMB)
@@ -304,15 +354,10 @@
     chains = [first_chain()] + [piece_chain(p) for p in range(1, PIECES)]
     next(chains[0])
 
-    for copy in handed[1]:
-        copy.wait_recv()
-    weight_piece(1, pooled_t, low[1])
-    next(chains[1])
-
-    def cross(i):
+    def cross(i, start):
         pair = slice(256 * i, 256 * i + 256)
-        for c in range(GROUP // 256):
-            rows = slice(256 * c, 256 * c + 256)
+        for c in range(HALF // 192):
+            rows = pl.ds(pl.multiple_of(start + 192 * c, 64), 192)
             inner2 = dot(low[0, rows, :], ew_ref[pair, :], ((1,), (1,)))
             back2 = dot(low[1, rows, :], rw_ref[pair, :], ((1,), (1,)))
             for u in range(2):
@@ -331,19 +376,26 @@
             value = dot(counts[t], spread[:, t * EMB : (t + 1) * EMB], ((1,), (0,)))
             owns[p][:, 16 * k : 16 * k + 16, :] = value.reshape(NREP, 16, EMB)
 
-    cross(0)
-    cross(1)
+    cross(0, mine)
+    cross(1, mine)
+    handed[1].wait_recv()
+    weight_piece(1, pooled_t, low[1])
     next(chains[1])
+    cross(0, theirs)
+    cross(1, theirs)
     table_piece(2)
     next(chains[2])
     next(chains[1])
     next(chains[0])
-    cross(2)
-    cross(3)
+    cross(2, mine)
+    cross(3, mine)
+    next(chains[1])
     next(chains[2])
-    next(chains[1])
+    cross(2, theirs)
+    cross(3, theirs)
     table_piece(3)
     next(chains[3])
+    next(chains[1])
     next(chains[2])
     next(chains[0])
     next(chains[3])
@@ -357,8 +409,8 @@
     finish(1)
     next(chains[0])
     zl_stage(3, next(chains[3]))
-    arrived = next(chains[0])
-    last[0] = own_a[zl, y] + arrived[0][...].astype(F32) + arrived[1][...].astype(F32)
+    ends = next(chains[0])
+    last[0] = own_a[zl, y] + ends[0][...].astype(F32) + ends[1][...].astype(F32)
     finish(0)
     finish(2)
     finish(3)
@@ -409,11 +461,11 @@
             pltpu.VMEM((GROUP, TABLES), F32),
             pltpu.VMEM((TABLES, GROUP), F32),
             pltpu.VMEM((TABLES, EMB), F32),
-            pltpu.VMEM((2, HALF, RANK), F32),
-            pltpu.VMEM((2, HALF, RANK), F32),
+            pltpu.VMEM((2, HALF, RANK), BF16),
+            pltpu.VMEM((2, HALF, RANK), BF16),
             pltpu.VMEM((2, NX, CHUNK, RANK), F32),
-            pltpu.VMEM((2, NX - 1, CHUNK, RANK), BF16),
-            pltpu.VMEM((2, NX - 1, CHUNK, RANK), BF16),
+            pltpu.VMEM((2, 2, NX // 2, CHUNK, RANK), BF16),
+            pltpu.VMEM((2, 2, NX // 2, CHUNK, RANK), BF16),
             pltpu.VMEM((2, CHUNK, RANK), BF16),
             pltpu.VMEM((2, CHUNK, RANK), BF16),
             pltpu.VMEM((2, GROUP, RANK), BF16),

time: 88.6 us -> 85 us (0.959)
  the two profiles are of different devices: /device:TPU:2 before, /device:TPU:4 now
where the time goes in v3:
time: 85 us; the launch traced here: 84.9 us
  Pallas kernels  80.7 us (95%)
  local copies, waits for them, and re-layouts  3.51 us (4%)
    pallas_call x1, Pallas kernels, body(): pl.pallas_call(kernel, out_shape=tuple((pltpu.VMEM(*k) for k in kept)), i...  80.7 us
    unnamed x5, local copies, waits for them, and re-layouts  3.51 us

profile of v3, /device:TPU:4, one launch (start us, length us, event | category | flops | bytes accessed | tf_op | source)
XLA Modules:
  0.0 84.9 jit_solution(11354446575053289786)
XLA Ops:
  0.6 80.7 %shard_map.110 = (bf16[768,1024]{1,0:T(8,128)(2,1)S(1)}, f32[32,256]{1,0:T(8,128)S(1)}, f32[32,256]{1,0:T(8,128)S(1)}, f32[1,32]{1,0:T(1,128)S(1)}, f32[8,16,128]{2,1,0:T(8,128)S(1)}) custom-call(s32[8,4,768]{2,1,0:T(4,128)} %bitcast.5, s32[8,768]{1,0:T(8,128)} %bitcast.6, bf16[8,512,128]{2,1,0:T(8,128)(2,1)} %tables_hbm.1, bf16[768,1024]{1,0:T(8,128)(2,1)} %cot_hbm.1, ...), custom_call_target="tpu_custom_call" | custom-call | flops 5368709120 | bytes 8388608 | tf_op jit(solution)/shard_map/pallas_call | solution.py:440
  81.4 1.1 %copy.17 = bf16[768,1024]{1,0:T(8,128)(2,1)} copy(bf16[768,1024]{1,0:T(8,128)(2,1)S(1)} %get-tuple-element.15) | data formatting | bytes 3145728
  82.5 0.5 copy.20
  83.0 0.6 copy.18
  83.6 0.6 copy.19
  84.3 0.6 copy.21

commit v4 on v3

--- a/solution.py
+++ b/solution.py
@@ -17,6 +17,7 @@
 TPP = 4
 WIDE = 64
 TALL = 80
+FAR_FIRST = (4, 3, 5, 2, 6, 1, 7)
 MESH = pl.DeviceIdType.MESH
 BF16 = jnp.bfloat16
 F32 = jnp.float32
@@ -78,6 +79,7 @@
 
     y_side = (rep_at(lax.rem(y + 1, NY), zl), rep_at(lax.rem(y + NY - 1, NY), zl))
     other_core, other_zh = mp_at(x, zh, 1 - core), mp_at(x, 1 - zh, core)
+    y_peer = [rep_at(lax.rem(y + o, NY), zl) for o in range(1, NY)]
     zl_peer = [rep_at(y, lax.rem(zl + o, NZL)) for o in range(1, NZL)]
 
     x_at = [
@@ -87,7 +89,7 @@
     x_dev = [[None] + [mp_at(x_at[way][o], zh, core) for o in (1, 2)] for way in range(2)]
 
     barrier = pltpu.get_barrier_semaphore()
-    greeted = [*x_dev[0][1:], *x_dev[1][1:], *y_side, other_core, other_zh, *zl_peer]
+    greeted = [*x_dev[0][1:], *x_dev[1][1:], *y_peer, other_core, other_zh, *zl_peer]
     for device in greeted:
         pl.semaphore_signal(barrier, inc=1, device_id=device, device_id_type=MESH)
 
@@ -240,7 +242,6 @@
     gather_second(0)
     gather_second(1)
     gather_last(0)
-    gather_last(1)
 
     def reduce_chain(part, n, me, own, send, recv, sides):
         count = [hops(part, way, n) for way in range(2)]
@@ -301,13 +302,16 @@
         second.wait_recv()
         for k in range(NY):
             own_a[zl, k] += near_recv[1, k].astype(F32) + across_recv[k].astype(F32)
-        yield from reduce_chain(
-            0, NY, y,
-            lambda dest: own_a[zl, dest],
-            lambda way, step: send_a.at[way, step],
-            lambda way, step: recv_a.at[way, step],
-            y_side,
-        )
+        rounds = []
+        for o in FAR_FIRST:
+            send_a[o - 1] = own_a[zl, lax.rem(y + o, NY)].astype(BF16)
+            rounds.append(links.copy(send_a.at[o - 1], recv_a.at[o - 1], y_peer[o - 1]))
+        yield
+        total = own_a[zl, y]
+        for copy, o in zip(rounds, FAR_FIRST, strict=True):
+            copy.wait_recv()
+            total = total + recv_a[o - 1].astype(F32)
+        yield total
 
     last = [None] * PIECES
     spreads = [[] for _ in range(PIECES)]
@@ -376,6 +380,7 @@
             value = dot(counts[t], spread[:, t * EMB : (t + 1) * EMB], ((1,), (0,)))
             owns[p][:, 16 * k : 16 * k + 16, :] = value.reshape(NREP, 16, EMB)
 
+    gather_last(1)
     cross(0, mine)
     cross(1, mine)
     handed[1].wait_recv()
@@ -386,31 +391,26 @@
     table_piece(2)
     next(chains[2])
     next(chains[1])
-    next(chains[0])
-    cross(2, mine)
-    cross(3, mine)
-    next(chains[1])
-    next(chains[2])
-    cross(2, theirs)
-    cross(3, theirs)
+    for start in (mine, theirs):
+        cross(2, start)
+        cross(3, start)
     table_piece(3)
     next(chains[3])
+    next(chains[2])
     next(chains[1])
+    next(chains[0])
+    next(chains[3])
+    next(chains[2])
+    next(chains[1])
+    next(chains[3])
     next(chains[2])
     next(chains[0])
-    next(chains[3])
     zl_stage(1, next(chains[1]))
-    next(chains[2])
-    next(chains[0])
     next(chains[3])
     zl_stage(2, next(chains[2]))
-    next(chains[0])
-    next(chains[3])
     finish(1)
-    next(chains[0])
+    last[0] = next(chains[0])
     zl_stage(3, next(chains[3]))
-    ends = next(chains[0])
-    last[0] = own_a[zl, y] + ends[0][...].astype(F32) + ends[1][...].astype(F32)
     finish(0)
     finish(2)
     finish(3)
@@ -419,12 +419,8 @@
 
 
 def hand_out(*refs):
-    sems = refs[10]
-    copies = [pltpu.make_async_copy(refs[i], refs[5 + i], sems.at[i]) for i in range(5)]
-    for copy in copies:
-        copy.start()
-    for copy in copies:
-        copy.wait()
+    for i in range(4):
+        refs[4 + i][...] = refs[i][...]
 
 
 def body(tables, feature_ids, bag_lengths, reduce_weight, expand_weight, cross_bias, cotangent):
@@ -477,9 +473,9 @@
             pltpu.VMEM((2, NY, TALL, EMB), BF16),
             pltpu.VMEM((NY, TALL, EMB), BF16),
             pltpu.VMEM((NY, TALL, EMB), BF16),
-            pltpu.VMEM((2, NY // 2, TALL, EMB), BF16),
+            pltpu.VMEM((NY - 1, TALL, EMB), BF16),
             pltpu.VMEM((PIECES - 1, 2, NY // 2, NZL, WIDE, EMB), BF16),
-            pltpu.VMEM((2, NY // 2, TALL, EMB), BF16),
+            pltpu.VMEM((NY - 1, TALL, EMB), BF16),
             pltpu.VMEM((PIECES - 1, 2, NY // 2, NZL, WIDE, EMB), BF16),
             pltpu.VMEM((PIECES - 1, NZL - 1, WIDE, EMB), BF16),
             pltpu.VMEM((PIECES - 1, NZL - 1, WIDE, EMB), BF16),
@@ -501,7 +497,13 @@
         expand_weight,
         cross_bias.reshape(TABLES, EMB),
     )
-    crossed, grad_reduce, grad_expand, grad_bias, grad_tables = made
+    crossed = made[0]
+    grad_reduce, grad_expand, grad_bias, grad_tables = pl.pallas_call(
+        hand_out,
+        out_shape=tuple(jax.ShapeDtypeStruct(*k) for k in kept[1:]),
+        in_specs=[vmem] * 4,
+        out_specs=(vmem,) * 4,
+    )(*made[1:])
     return crossed, grad_reduce, grad_expand, grad_bias.reshape(-1), grad_tables
 
 

time: 85 us -> 84 us (0.988)
  the two profiles are of different devices: /device:TPU:4 before, /device:TPU:6 now
where the time goes in v4:
time: 84 us; the launch traced here: 83.8 us
  Pallas kernels  82 us (98%)
  local copies, waits for them, and re-layouts  1.17 us (1%)
    pallas_call x1, Pallas kernels, body(): pl.pallas_call(kernel, out_shape=tuple((pltpu.VMEM(*k) for k in kept)), i...  80.4 us

profile of v4, /device:TPU:6, one launch (start us, length us, event | category | flops | bytes accessed | tf_op | source)
XLA Modules:
  0.0 83.8 jit_solution(4889920824423721001)
XLA Ops:
  0.6 80.4 %shard_map.110 = (bf16[768,1024]{1,0:T(8,128)(2,1)S(1)}, f32[32,256]{1,0:T(8,128)S(1)}, f32[32,256]{1,0:T(8,128)S(1)}, f32[1,32]{1,0:T(1,128)S(1)}, f32[8,16,128]{2,1,0:T(8,128)S(1)}) custom-call(s32[8,4,768]{2,1,0:T(4,128)} %bitcast.4, s32[8,768]{1,0:T(8,128)} %bitcast.5, bf16[8,512,128]{2,1,0:T(8,128)(2,1)} %tables_hbm.1, bf16[768,1024]{1,0:T(8,128)(2,1)} %cot_hbm.1, ...), custom_call_target="tpu_custom_call" | custom-call | flops 5368709120 | bytes 8388608 | tf_op jit(solution)/shard_map/pallas_call | solution.py:436
  81.1 0.0 copy-start
  81.1 0.0 copy-start.1
  81.1 0.0 copy-start.2
  81.1 0.0 copy-start.3
  81.1 1.1 %copy.13 = bf16[768,1024]{1,0:T(8,128)(2,1)} copy(bf16[768,1024]{1,0:T(8,128)(2,1)S(1)} %get-tuple-element.23) | data formatting | bytes 3145728
  82.3 0.0 copy-done
  82.3 0.0 copy-done.1
  82.3 0.0 copy-done.2
  82.3 0.0 copy-done.3
  82.3 1.5 %shard_map.111 = (f32[32,256]{1,0:T(8,128)}, f32[32,256]{1,0:T(8,128)}, f32[1,32]{1,0:T(1,128)}, f32[8,16,128]{2,1,0:T(8,128)}) custom-call(f32[32,256]{1,0:T(8,128)} %copy-done.1, f32[32,256]{1,0:T(8,128)} %copy-done.2, f32[1,32]{1,0:T(1,128)} %copy-done.3, f32[8,16,128]{2,1,0:T(8,128)} %copy-done), custom_call_target="tpu_custom_call" | custom-call | tf_op jit(solution)/shard_map/pallas_call | solution.py:501
Async XLA Ops:
  81.1 1.2 %copy-start = (f32[8,16,128]{2,1,0:T(8,128)}, f32[8,16,128]{2,1,0:T(8,128)S(1)}, u32[]{:S(2)}) copy-start(f32[8,16,128]{2,1,0:T(8,128)S(1)} %get-tuple-element.18.refs_3_) | copy-start | bytes 196612
  81.1 1.2 %copy-start.1 = (f32[32,256]{1,0:T(8,128)}, f32[32,256]{1,0:T(8,128)S(1)}, u32[]{:S(2)}) copy-start(f32[32,256]{1,0:T(8,128)S(1)} %get-tuple-element.15.refs_0_) | copy-start | bytes 98308
  81.1 1.2 %copy-start.2 = (f32[32,256]{1,0:T(8,128)}, f32[32,256]{1,0:T(8,128)S(1)}, u32[]{:S(2)}) copy-start(f32[32,256]{1,0:T(8,128)S(1)} %get-tuple-element.16.refs_1_) | copy-start | bytes 98308
  81.1 1.2 %copy-start.3 = (f32[1,32]{1,0:T(1,128)}, f32[1,32]{1,0:T(1,128)S(1)}, u32[]{:S(2)}) copy-start(f32[1,32]{1,0:T(1,128)S(1)} %get-tuple-element.17.refs_2_) | copy-start | bytes 388

commit v5 on v4

--- a/solution.py
+++ b/solution.py
@@ -17,6 +17,7 @@
 TPP = 4
 WIDE = 64
 TALL = 80
+LINES = NY * WIDE
 FAR_FIRST = (4, 3, 5, 2, 6, 1, 7)
 MESH = pl.DeviceIdType.MESH
 BF16 = jnp.bfloat16
@@ -291,23 +292,35 @@
         across = lax.rem(zl + 2, NZL)
         firsts = []
         for k, keeper in enumerate((lax.rem(near + 2, NZL), near)):
-            near_send[k] = own_a[keeper].astype(BF16)
+            near_send[k, 0:LINES] = own_a[keeper].reshape(LINES, EMB).astype(BF16)
+            near_send[k, LINES:] = jnp.concatenate([biases[...]] * 2, axis=0).astype(BF16)
             firsts.append(links.copy(near_send.at[k], near_recv.at[k], rep_at(y, near)))
         yield
         firsts[0].wait_recv()
-        across_send[...] = (own_a[across] + near_recv[0].astype(F32)).astype(BF16)
+        across_send[0:LINES] = (
+            own_a[across].reshape(LINES, EMB) + near_recv[0, 0:LINES].astype(F32)
+        ).astype(BF16)
+        biases[...] += near_recv[0, LINES:].astype(F32)[0:TABLES]
+        across_send[LINES:] = jnp.concatenate([biases[...]] * 2, axis=0).astype(BF16)
         second = links.copy(across_send, across_recv, rep_at(y, across))
         yield
         firsts[1].wait_recv()
         second.wait_recv()
         for k in range(NY):
-            own_a[zl, k] += near_recv[1, k].astype(F32) + across_recv[k].astype(F32)
+            rows = slice(k * WIDE, (k + 1) * WIDE)
+            own_a[zl, k] += near_recv[1, rows].astype(F32) + across_recv[rows].astype(F32)
+        biases[...] += across_recv[LINES:].astype(F32)[0:TABLES]
+
+        def tall(where):
+            line = jnp.broadcast_to(biases[pl.ds(where, 1), :], (TALL - WIDE, EMB))
+            return jnp.concatenate([own_a[zl, where], line], axis=0)
+
         rounds = []
         for o in FAR_FIRST:
-            send_a[o - 1] = own_a[zl, lax.rem(y + o, NY)].astype(BF16)
+            send_a[o - 1] = tall(lax.rem(y + o, NY)).astype(BF16)
             rounds.append(links.copy(send_a.at[o - 1], recv_a.at[o - 1], y_peer[o - 1]))
         yield
-        total = own_a[zl, y]
+        total = tall(y)
         for copy, o in zip(rounds, FAR_FIRST, strict=True):
             copy.wait_recv()
             total = total + recv_a[o - 1].astype(F32)
@@ -350,10 +363,6 @@
                 gtables_ref[(p - 2) * TPP + t] = total[16 * t : 16 * t + 16, :]
 
     handed[0].wait_recv()
-    for t in range(TABLES):
-        own_a[:, t, 64:80, :] = jnp.broadcast_to(
-            biases[t : t + 1, :].reshape(1, 1, EMB), (NZL, 16, EMB)
-        )
     weight_piece(0, gb_t, low[0])
     chains = [first_chain()] + [piece_chain(p) for p in range(1, PIECES)]
     next(chains[0])
@@ -465,14 +474,14 @@
             pltpu.VMEM((2, CHUNK, RANK), BF16),
             pltpu.VMEM((2, CHUNK, RANK), BF16),
             pltpu.VMEM((2, GROUP, RANK), BF16),
-            pltpu.VMEM((NZL, NY, TALL, EMB), F32),
+            pltpu.VMEM((NZL, NY, WIDE, EMB), F32),
             pltpu.VMEM((NREP, WIDE, EMB), F32),
             pltpu.VMEM((NREP, WIDE, EMB), F32),
             pltpu.VMEM((NREP, WIDE, EMB), F32),
-            pltpu.VMEM((2, NY, TALL, EMB), BF16),
-            pltpu.VMEM((2, NY, TALL, EMB), BF16),
-            pltpu.VMEM((NY, TALL, EMB), BF16),
-            pltpu.VMEM((NY, TALL, EMB), BF16),
+            pltpu.VMEM((2, LINES + 16, EMB), BF16),
+            pltpu.VMEM((2, LINES + 16, EMB), BF16),
+            pltpu.VMEM((LINES + 16, EMB), BF16),
+            pltpu.VMEM((LINES + 16, EMB), BF16),
             pltpu.VMEM((NY - 1, TALL, EMB), BF16),
             pltpu.VMEM((PIECES - 1, 2, NY // 2, NZL, WIDE, EMB), BF16),
             pltpu.VMEM((NY - 1, TALL, EMB), BF16),

time: 84 us -> 83.9 us (level)
  no operation moved by 1% of the time
where the time goes in v5:
time: 83.9 us; the launch traced here: 83.7 us
  Pallas kernels  81.9 us (98%)
  local copies, waits for them, and re-layouts  1.17 us (1%)
    pallas_call x1, Pallas kernels, body(): pl.pallas_call(kernel, out_shape=tuple((pltpu.VMEM(*k) for k in kept)), i...  80.4 us

profile of v5, /device:TPU:6, one launch (start us, length us, event | category | flops | bytes accessed | tf_op | source)
XLA Modules:
  0.0 83.7 jit_solution(1729781728354911564)
XLA Ops:
  0.6 80.4 %shard_map.110 = (bf16[768,1024]{1,0:T(8,128)(2,1)S(1)}, f32[32,256]{1,0:T(8,128)S(1)}, f32[32,256]{1,0:T(8,128)S(1)}, f32[1,32]{1,0:T(1,128)S(1)}, f32[8,16,128]{2,1,0:T(8,128)S(1)}) custom-call(s32[8,4,768]{2,1,0:T(4,128)} %bitcast.4, s32[8,768]{1,0:T(8,128)} %bitcast.5, bf16[8,512,128]{2,1,0:T(8,128)(2,1)} %tables_hbm.1, bf16[768,1024]{1,0:T(8,128)(2,1)} %cot_hbm.1, ...), custom_call_target="tpu_custom_call" | custom-call | flops 5368709120 | bytes 8388608 | tf_op jit(solution)/shard_map/pallas_call | solution.py:445
  81.0 0.0 copy-start
  81.0 0.0 copy-start.1
  81.0 0.0 copy-start.2
  81.0 0.0 copy-start.3
  81.0 1.1 %copy.13 = bf16[768,1024]{1,0:T(8,128)(2,1)} copy(bf16[768,1024]{1,0:T(8,128)(2,1)S(1)} %get-tuple-element.23) | data formatting | bytes 3145728
  82.2 0.0 copy-done
  82.2 0.0 copy-done.1
  82.2 0.0 copy-done.2
  82.2 0.0 copy-done.3
  82.2 1.5 %shard_map.111 = (f32[32,256]{1,0:T(8,128)}, f32[32,256]{1,0:T(8,128)}, f32[1,32]{1,0:T(1,128)}, f32[8,16,128]{2,1,0:T(8,128)}) custom-call(f32[32,256]{1,0:T(8,128)} %copy-done.1, f32[32,256]{1,0:T(8,128)} %copy-done.2, f32[1,32]{1,0:T(1,128)} %copy-done.3, f32[8,16,128]{2,1,0:T(8,128)} %copy-done), custom_call_target="tpu_custom_call" | custom-call | tf_op jit(solution)/shard_map/pallas_call | solution.py:510
Async XLA Ops:
  81.0 1.2 %copy-start = (f32[8,16,128]{2,1,0:T(8,128)}, f32[8,16,128]{2,1,0:T(8,128)S(1)}, u32[]{:S(2)}) copy-start(f32[8,16,128]{2,1,0:T(8,128)S(1)} %get-tuple-element.18.refs_3_) | copy-start | bytes 196612
  81.0 1.2 %copy-start.1 = (f32[32,256]{1,0:T(8,128)}, f32[32,256]{1,0:T(8,128)S(1)}, u32[]{:S(2)}) copy-start(f32[32,256]{1,0:T(8,128)S(1)} %get-tuple-element.15.refs_0_) | copy-start | bytes 98308
  81.0 1.2 %copy-start.2 = (f32[32,256]{1,0:T(8,128)}, f32[32,256]{1,0:T(8,128)S(1)}, u32[]{:S(2)}) copy-start(f32[32,256]{1,0:T(8,128)S(1)} %get-tuple-element.16.refs_1_) | copy-start | bytes 98308
  81.0 1.2 %copy-start.3 = (f32[1,32]{1,0:T(1,128)}, f32[1,32]{1,0:T(1,128)S(1)}, u32[]{:S(2)}) copy-start(f32[1,32]{1,0:T(1,128)S(1)} %get-tuple-element.17.refs_2_) | copy-start | bytes 388
